TPU v7x, 32 devices: a whole 2x2x4 slice. The times are simulated.
32 devices in a mesh: groups: 1, ctx: 4 (over y, x), ep: 8 (over z, core).
Axes of the slice: x: 2, y: 2, z: 4, core: 2. Of those that a mesh axis runs over, the one named last changes fastest.
Arguments:
- query: bfloat16 [8, 256, 4096], P(('groups', 'ep'), 'ctx'), may hold values from -120 to 120
- keys: bfloat16 [8, 256, 256], P(('groups', 'ep'), 'ctx'), may hold values from -6 to 6
- values: bfloat16 [8, 256, 256], P(('groups', 'ep'), 'ctx'), may hold values from -6 to 6
- kept_pos: int32 [8, 256], P(('groups', 'ep'), 'ctx'), may hold values from 0 to 1020, as said below
- hidden: bfloat16 [4096, 2048], P(('groups', 'ctx', 'ep')), may hold values from -6 to 6
- norm_gain: float32 [2048], replicated, may hold values from 0.1 to 1.9
- routes: int32 [4096, 4], P(('groups', 'ctx', 'ep')), may hold values from 0 to 7, all different within a row; in each aligned block of 128 rows (0 to 127, 128 to 255, ...) at most 80 rows name the same one
- route_weight: float32 [4096, 4], P(('groups', 'ctx', 'ep')), may hold values from 0.2 to 1
- capacity: int32 [8], replicated, may hold values from 40 to 80, as said below
- w_gate: bfloat16 [8, 2048, 768], P('ep', 'ctx'), may hold values from -0.125 to 0.125
- w_up: bfloat16 [8, 2048, 768], P('ep', 'ctx'), may hold values from -0.125 to 0.125
- w_down: bfloat16 [8, 768, 2048], P('ep', 'ctx'), may hold values from -0.21875 to 0.21875
Outputs:
- attended: bfloat16 [8, 256, 4096], P(('groups', 'ep'), 'ctx')
- mixed: bfloat16 [4096, 2048], P(('groups', 'ctx', 'ep'))
Inputs may be any that keep to these rules, and one draw needn't show every extreme that they name: `kept_pos`: positions are all different within a sequence; every sequence has position 0 and position 1020. `routes`: in the rows of one device no expert is named more than 80 times. `capacity`: some expert has exactly 80.
All inputs are finite; a program needn't handle non-finite values.
Results may differ from a plain program's by a relative error of at most 0.0055.
Values may be sent and summed in bfloat16 or wider, within the bound.
A program may use at most 64 MiB of HBM per device.

v0:
```python
import math

import jax
import jax.numpy as jnp
from jax import lax
from jax.sharding import PartitionSpec as P

HEADS = 32
KVH = 2
HD = 128


def attention_section(query, keys, values, kept_pos):
    row_count = query.shape[1]
    group_size = HEADS // KVH
    score_scale = 1.0 / math.sqrt(HD)
    every_pos = lax.all_gather(kept_pos, "ctx", axis=1, tiled=True)[0]
    row_pos = jnp.tile(kept_pos[0], group_size)
    grouped = (
        query[0]
        .reshape(row_count, KVH, group_size, HD)
        .transpose(1, 2, 0, 3)
        .reshape(KVH, group_size * row_count, HD)
    )
    start_max = jnp.full((KVH, group_size * row_count), -1e30, jnp.float32)
    start_sum = jnp.zeros((KVH, group_size * row_count), jnp.float32)
    start_out = jnp.zeros((KVH, group_size * row_count, HD), jnp.float32)
    carry = (start_max, start_sum, start_out)
    start = jnp.int32(0)
    key_piece = lax.all_gather(keys, "ctx", axis=1, tiled=True)
    value_piece = lax.all_gather(values, "ctx", axis=1, tiled=True)
    piece_len = key_piece.shape[1]
    block_len = math.gcd(piece_len, 256)
    for offset in range(0, piece_len, block_len):
        key_block = key_piece[0, offset : offset + block_len]
        value_block = value_piece[0, offset : offset + block_len]
        running_max, running_sum, running_out = carry
        attend_block_len = key_block.shape[0]
        key_pos = lax.dynamic_slice_in_dim(every_pos, start + offset, attend_block_len, 0)
        key_heads = key_block.reshape(attend_block_len, KVH, HD)
        value_heads = value_block.reshape(attend_block_len, KVH, HD)
        scores = (
            jnp.einsum("kqd,nkd->kqn", grouped, key_heads, preferred_element_type=jnp.float32)
            * score_scale
        )
        scores = jnp.where((key_pos[None, :] <= row_pos[:, None])[None], scores, -jnp.inf)
        fresh_max = jnp.maximum(running_max, jnp.max(scores, axis=-1))
        decay_now = jnp.exp(running_max - fresh_max)
        weights = jnp.exp(scores - fresh_max[..., None])
        running_sum = running_sum * decay_now + jnp.sum(weights, axis=-1)
        running_out = running_out * decay_now[..., None] + jnp.einsum(
            "kqn,nkd->kqd",
            weights.astype(jnp.bfloat16),
            value_heads,
            preferred_element_type=jnp.float32,
        )
        carry = (fresh_max, running_sum, running_out)
    final_max, final_sum, final_out = carry
    result = (
        (final_out / final_sum[..., None])
        .reshape(KVH, group_size, row_count, HD)
        .transpose(2, 0, 1, 3)
    )
    return result.reshape(row_count, HEADS * HD).astype(jnp.bfloat16)[None]


def expert_section(hidden, norm_gain, routes, route_weight, capacity, w_gate, full_weights):
    tok_rows, model_width = hidden.shape
    route_count = routes.shape[1]
    experts = capacity.shape[0]
    local_count = w_gate.shape[0]
    owners = experts // local_count
    slot_cap = min(tok_rows, max(2, 5 * tok_rows * route_count // (4 * experts)))
    residual = hidden.astype(jnp.float32)
    normed = (
        residual
        * lax.rsqrt(jnp.mean(residual * residual, axis=-1, keepdims=True) + 1e-06)
        * norm_gain
    ).astype(jnp.bfloat16)
    flat_ids = routes.reshape(-1)
    onehot = (flat_ids[:, None] == jnp.arange(experts, dtype=jnp.int32)[None, :]).astype(jnp.int32)
    rank_of = jnp.sum((jnp.cumsum(onehot, axis=0) - onehot) * onehot, axis=1)
    limit_of = jnp.sum(onehot * capacity[None, :], axis=1)
    kept_mask = rank_of < limit_of
    slot_of = jnp.where(kept_mask, flat_ids * slot_cap + rank_of, -1)
    slot_grid = slot_of.reshape(tok_rows, route_count)
    dispatch_map = jnp.any(
        slot_grid[None, :, :] == jnp.arange(experts * slot_cap, dtype=jnp.int32)[:, None, None],
        axis=2,
    ).astype(jnp.bfloat16)
    outgoing = (
        jnp.dot(dispatch_map, normed, preferred_element_type=jnp.float32)
        .astype(jnp.bfloat16)
        .reshape(experts, slot_cap, model_width)
    )
    incoming = lax.all_to_all(outgoing, "ep", split_axis=0, concat_axis=0, tiled=True)
    received = (
        incoming.reshape(owners, local_count, slot_cap, model_width)
        .transpose(1, 0, 2, 3)
        .reshape(local_count, owners * slot_cap, model_width)
    )
    full_gate, full_up, full_down = full_weights
    gate_sum = jnp.einsum("erd,edf->erf", received, full_gate, preferred_element_type=jnp.float32)
    up_sum = jnp.einsum("erd,edf->erf", received, full_up, preferred_element_type=jnp.float32)
    hidden_act = (jax.nn.silu(gate_sum) * up_sum).astype(jnp.bfloat16)
    result = jnp.einsum("erf,efd->erd", hidden_act, full_down, preferred_element_type=jnp.float32)
    answer = (
        result.astype(jnp.bfloat16)
        .reshape(local_count, owners, slot_cap, model_width)
        .transpose(1, 0, 2, 3)
        .reshape(experts, slot_cap, model_width)
    )
    returned = lax.all_to_all(answer, "ep", split_axis=0, concat_axis=0, tiled=True)
    flat_out = returned.reshape(experts * slot_cap, model_width)
    picked = flat_out[jnp.maximum(slot_of, 0)].astype(jnp.float32)
    share_of = route_weight.reshape(-1) * kept_mask.astype(jnp.float32)
    contrib = jnp.sum(
        (picked * share_of[:, None]).reshape(tok_rows, route_count, model_width), axis=1
    )
    return (residual + contrib).astype(jnp.bfloat16)


def body(
    query,
    keys,
    values,
    kept_pos,
    hidden,
    norm_gain,
    routes,
    route_weight,
    capacity,
    w_gate,
    w_up,
    w_down,
):
    full_weights = (
        lax.all_gather(w_gate, "ctx", axis=1, tiled=True),
        lax.all_gather(w_up, "ctx", axis=1, tiled=True),
        lax.all_gather(w_down, "ctx", axis=1, tiled=True),
    )
    attended = attention_section(query, keys, values, kept_pos)
    mixed = expert_section(hidden, norm_gain, routes, route_weight, capacity, w_gate, full_weights)
    return (attended, mixed)


def solution(mesh):
    placed = (
        P(("groups", "ep"), "ctx", None),
        P(("groups", "ep"), "ctx", None),
        P(("groups", "ep"), "ctx", None),
        P(("groups", "ep"), "ctx"),
        P(("groups", "ctx", "ep"), None),
        P(),
        P(("groups", "ctx", "ep"), None),
        P(("groups", "ctx", "ep"), None),
        P(),
        P("ep", "ctx", None),
        P("ep", "ctx", None),
        P("ep", "ctx", None),
    )
    return jax.shard_map(
        body,
        mesh=mesh,
        in_specs=placed,
        out_specs=(P(("groups", "ep"), "ctx", None), P(("groups", "ctx", "ep"), None)),
        check_vma=False,
    )
```

profile of v0, /device:TPU:0, one launch (start us, length us, event | category | flops | bytes accessed | tf_op | source)
XLA Modules:
  0.0 244.1 jit_solution(15927636938205664320)
XLA Ops:
  9.7 1.1 reduce-window.6
  12.1 0.8 copy.52
  13.4 2.4 convolution_convert_fusion.1
  15.8 6.3 %all-to-all-start = ((bf16[8,80,2048]{2,1,0:T(8,128)(2,1)}), bf16[8,80,2048]{2,1,0:T(8,128)(2,1)S(1)}, u32[]{:S(2)}, u32[]{:S(2)}) async-start(bf16[8,80,2048]{2,1,0:T(8,128)(2,1)} %bitcast.10), calls=%async_computation | async-start | bytes 5242880 | tf_op jit(solution)/shard_map/all_to_all | solution.py:96
  22.8 59.6 %all-to-all-done = bf16[8,80,2048]{2,1,0:T(8,128)(2,1)S(1)} async-done(((bf16[8,80,2048]{2,1,0:T(8,128)(2,1)}), bf16[8,80,2048]{2,1,0:T(8,128)(2,1)S(1)}, u32[]{:S(2)}, u32[]{:S(2)}) %all-to-all-start) | async-done | bytes 2621472 | tf_op jit(solution)/shard_map/all_to_all | solution.py:96
  82.4 5.9 %fusion.3 = f32[640,768]{1,0:T(8,128)} fusion(bf16[640,2048]{1,0:T(8,128)(2,1)S(1)} %bitcast.53, bf16[1,2048,768]{2,1,0:T(8,128)(2,1)} %all-gather.4.cloned.1.call-done), kind=kOutput, calls=%fused_computation.7 | convolution fusion | flops 2013265920 | bytes 7733248 | tf_op jit(solution)/shard_map/erd,edf->erf/dot_general | solution.py:103
  88.3 14.2 %all-gather.6.cloned.1.call-done = bf16[1,2048,768]{2,1,0:T(8,128)(2,1)} async-done(((bf16[1,512,768]{2,1,0:T(8,128)(2,1)}), bf16[1,2048,768]{2,1,0:T(8,128)(2,1)}) %all-gather.6.cloned.1.call-update) | async-done | bytes 3145744 | tf_op jit(solution)/shard_map/all_gather | solution.py:139
  102.4 45.9 %all-gather.8.cloned.1.call-done = bf16[1,768,2048]{2,1,0:T(8,128)(2,1)} async-done(((bf16[1,192,2048]{2,1,0:T(8,128)(2,1)}), bf16[1,768,2048]{2,1,0:T(8,128)(2,1)}) %all-gather.8.cloned.1.call-update) | async-done | bytes 3145744 | tf_op jit(solution)/shard_map/all_gather | solution.py:140
  148.3 9.8 %convolution_convert_fusion = bf16[640,2048]{1,0:T(8,128)(2,1)} fusion(bf16[1,768,2048]{2,1,0:T(8,128)(2,1)} %all-gather.8.cloned.1.call-done, f32[640,768]{1,0:T(8,128)} %fusion.3, bf16[640,2048]{1,0:T(8,128)(2,1)S(1)} %bitcast.54, bf16[1,2048,768]{2,1,0:T(8,128)(2,1)} %all-gather.6.cloned.1.call-done), kind=kOutput, calls=%fused_computation.2 | convolution fusion | flops 4030791680 | bytes 13500416 | tf_op jit(solution)/shard_map/erf,efd->erd/dot_general | solution.py:106
  158.1 4.7 %all-to-all-start.1 = ((bf16[8,80,2048]{2,1,0:T(8,128)(2,1)}), bf16[8,80,2048]{2,1,0:T(8,128)(2,1)S(1)}, u32[]{:S(2)}, u32[]{:S(2)}) async-start(bf16[8,80,2048]{2,1,0:T(8,128)(2,1)} %bitcast.52), calls=%async_computation.1 | async-start | bytes 5242880 | tf_op jit(solution)/shard_map/all_to_all | solution.py:113
  163.1 1.1 copy.56
  164.2 1.0 copy.41
  165.2 8.4 %all_gather.22 = bf16[1,256,256]{2,1,0:T(8,128)(2,1)S(1)} all-gather(bf16[1,64,256]{2,1,0:T(8,128)(2,1)S(1)} %copy-done.2), channel_id=1, replica_groups=mesh['groups'=1,'ctx'=4,'ep'=8] {'ctx'}, dimensions={1}, use_global_device_ids=true | all-gather | bytes 163840 | tf_op jit(solution)/shard_map/all_gather | solution.py:30
  173.7 7.5 %all_gather.23 = bf16[1,256,256]{2,1,0:T(8,128)(2,1)S(1)} all-gather(bf16[1,64,256]{2,1,0:T(8,128)(2,1)S(1)} %copy-done.3), channel_id=1, replica_groups=mesh['groups'=1,'ctx'=4,'ep'=8] {'ctx'}, dimensions={1}, use_global_device_ids=true | all-gather | bytes 163840 | tf_op jit(solution)/shard_map/all_gather | solution.py:31
  183.5 7.5 %all-reduce = s32[256]{0:T(256)S(1)} all-reduce(s32[256]{0:T(256)S(1)} %bitcast_dynamic-update-slice_fusion), channel_id=1, replica_groups=mesh['groups'=1,'ctx'=4,'ep'=8] {'ctx'}, use_global_device_ids=true, to_apply=%add | all-reduce | flops 256 | bytes 2048
  191.2 1.7 fusion.5
  193.4 1.3 fusion.12
  194.8 1.1 copy.47
  195.9 2.1 convert_element_type.62
  198.0 25.2 %all-to-all-done.1 = bf16[8,80,2048]{2,1,0:T(8,128)(2,1)S(1)} async-done(((bf16[8,80,2048]{2,1,0:T(8,128)(2,1)}), bf16[8,80,2048]{2,1,0:T(8,128)(2,1)S(1)}, u32[]{:S(2)}, u32[]{:S(2)}) %all-to-all-start.1) | async-done | bytes 2621472 | tf_op jit(solution)/shard_map/all_to_all | solution.py:113
  223.1 3.3 %gather_fusion = bf16[512,2048]{1,0:T(8,128)(2,1)} fusion(bf16[640,2048]{1,0:T(8,128)(2,1)S(1)} %bitcast.51, s32[1024]{0:T(1024)S(1)} %pad_clamp_fusion), kind=kCustom, calls=%fused_computation | custom fusion | bytes 4196352 | tf_op jit(solution)/shard_map/gather | solution.py:115
  226.5 4.8 %reshape.199 = f32[128,4,2048]{2,1,0:T(4,128)} reshape(bf16[512,2048]{1,0:T(8,128)(2,1)} %gather_fusion) | data formatting | bytes 6291456 | tf_op jit(solution)/shard_map/convert_element_type | solution.py:115
  231.2 5.4 %multiply_reduce_fusion = f32[128,2048]{1,0:T(8,128)S(1)} fusion(f32[128,4,2048]{2,1,0:T(4,128)} %reshape.199, f32[128,4]{1,0:T(8,128)S(1)} %get-tuple-element.4), kind=kLoop, calls=%fused_computation.1 | loop fusion | flops 1835008 | bytes 5244928 | tf_op jit(solution)/shard_map/reduce_sum | solution.py:117
  236.6 0.9 fusion.16
  (51 shorter events, 7.5 us)
Async XLA Ops:
  7.2 6.0 %copy-start = (bf16[128,2048]{1,0:T(8,128)(2,1)S(1)}, bf16[128,2048]{1,0:T(8,128)(2,1)}, u32[]{:S(2)}) copy-start(bf16[128,2048]{1,0:T(8,128)(2,1)} %param.16) | copy-start | bytes 1572868
  7.2 6.2 %copy-start.4 = (f32[2048]{0:T(1024)S(1)}, f32[2048]{0:T(1024)}, u32[]{:S(2)}) copy-start(f32[2048]{0:T(1024)} %param.17) | copy-start | bytes 24580
  7.2 75.2 %all-gather.4.cloned.1.call-start = ((), (), s32[]{:S(2)}) async-start(), calls=%async_computation.2 | async-start | bytes 3932160 | tf_op jit(solution)/shard_map/all_gather | solution.py:138
  7.9 94.5 %all-gather.6.cloned.1.call-start = ((), (), s32[]{:S(2)}) async-start(), calls=%async_computation.3 | async-start | bytes 3932160 | tf_op jit(solution)/shard_map/all_gather | solution.py:139
  15.8 66.6 %all-to-all-start = ((bf16[8,80,2048]{2,1,0:T(8,128)(2,1)}), bf16[8,80,2048]{2,1,0:T(8,128)(2,1)S(1)}, u32[]{:S(2)}, u32[]{:S(2)}) async-start(bf16[8,80,2048]{2,1,0:T(8,128)(2,1)} %bitcast.10), calls=%async_computation | async-start | bytes 5242880 | tf_op jit(solution)/shard_map/all_to_all | solution.py:96
  22.1 126.2 %all-gather.8.cloned.1.call-start = ((), (), s32[]{:S(2)}) async-start(), calls=%async_computation.4 | async-start | bytes 3932160 | tf_op jit(solution)/shard_map/all_gather | solution.py:140
  158.1 4.9 %copy-start.5 = (s32[1,64]{1,0:T(1,128)S(1)}, s32[1,64]{1,0:T(1,128)}, u32[]{:S(2)}) copy-start(s32[1,64]{1,0:T(1,128)} %param.15) | copy-start | bytes 772
  158.1 65.0 %all-to-all-start.1 = ((bf16[8,80,2048]{2,1,0:T(8,128)(2,1)}), bf16[8,80,2048]{2,1,0:T(8,128)(2,1)S(1)}, u32[]{:S(2)}, u32[]{:S(2)}) async-start(bf16[8,80,2048]{2,1,0:T(8,128)(2,1)} %bitcast.52), calls=%async_computation.1 | async-start | bytes 5242880 | tf_op jit(solution)/shard_map/all_to_all | solution.py:113
  162.8 2.4 copy-start.2
  162.8 10.9 %copy-start.3 = (bf16[1,64,256]{2,1,0:T(8,128)(2,1)S(1)}, bf16[1,64,256]{2,1,0:T(8,128)(2,1)}, u32[]{:S(2)}) copy-start(bf16[1,64,256]{2,1,0:T(8,128)(2,1)} %param.14) | copy-start | bytes 98308
  162.9 19.2 %copy-start.6 = (u32[32]{0:T(128)S(1)}, u32[32]{0:T(128)}, u32[]{:S(2)}) copy-start(u32[32]{0:T(128)} %constant.44) | copy-start | bytes 388
  191.2 2.3 copy-start.1
Sparse Core Ops, SparseCore 0:
  9.9 46.6 all-gather.3
  58.4 43.9 all-gather.5
  104.3 43.9 all-gather.7
where the time goes:
time: 245 us; the launch traced here: 244 us
  waiting for transfers between devices  147 us (60%)
  blocking collectives  23.4 us (10%)
  matrix products  21.1 us (9%)
  local copies, waits for them, and re-layouts  17.5 us (7%)
  between operations  14.7 us (6%)
  starting transfers between devices  11.2 us (5%)
  other arithmetic  9.45 us (4%)
    all_to_all x1, waiting for transfers between devices, expert_section(): lax.all_to_all(outgoing, 'ep', split_axis=0, concat_axis=0, tiled=True)  59.6 us
    all_gather x1, waiting for transfers between devices, body(): lax.all_gather(w_down, 'ctx', axis=1, tiled=True)  45.9 us
    all_to_all x1, waiting for transfers between devices, expert_section(): lax.all_to_all(answer, 'ep', split_axis=0, concat_axis=0, tiled=True)  25.2 us
    all_gather x1, waiting for transfers between devices, body(): lax.all_gather(w_up, 'ctx', axis=1, tiled=True)  14.2 us
    dot_general x1, matrix products, expert_section(): jnp.einsum('erf,efd->erd', hidden_act, full_down, preferred_element_type=...  9.83 us
    all_gather x1, blocking collectives, attention_section(): key_piece = lax.all_gather(keys, 'ctx', axis=1, tiled=True)  8.41 us
    all_gather x1, blocking collectives, attention_section(): value_piece = lax.all_gather(values, 'ctx', axis=1, tiled=True)  7.51 us
    unnamed x1, blocking collectives  7.46 us
  transfers between devices with their start and end apart: 5, of which 4 were waited for; matrix products, arithmetic and copies ran while one was open for 10% of the time, Pallas kernels for 0%

commit v1 on v0

v1 whole, which is shorter than its diff:
```python
import functools
import math

import jax
import jax.numpy as jnp
from jax import lax
from jax.experimental import pallas as pl
from jax.experimental.pallas import tpu as pltpu
from jax.sharding import PartitionSpec as P

HEADS = 32
KVH = 2
HD = 128
STACK = 4
CHUNKS = 4
F32 = jnp.float32
BF16 = jnp.bfloat16


def kernel(
    n_ctx, n_ep, slots,
    q_ref, k_ref, v_ref, prow_ref, pcol_ref, hid_ref, gain_ref, rt_ref, wt_ref, cap_ref,
    wg_ref, wu_ref, wd_ref,
    att_ref, mix_ref,
    kb, vb, pb, tok, rb, xb, wgb, wub, wdb, gb, ab, yb, sib, ret, own,
    kv_s, kv_r, w_s, w_r, f_s, t_s, t_r, u_s, u_r, s_s, s_r, r_s, r_r,
):
    gi = lax.axis_index("groups")
    c = lax.axis_index("ctx")
    p = lax.axis_index("ep")
    n_z = n_ep // 2
    z, core = p // 2, p % 2
    sibling = z * 2 + (1 - core)
    square = n_ctx == 4
    rows = k_ref.shape[0]
    toks, width = hid_ref.shape
    experts = cap_ref.shape[0]
    ff = wg_ref.shape[1]
    cw = width // CHUNKS

    def dev(cc, pp):
        return (gi, cc, pp)

    barrier = pltpu.get_barrier_semaphore()
    for d in range(1, n_ctx):
        pl.semaphore_signal(barrier, inc=1, device_id=dev(lax.rem(c + d, n_ctx), p), device_id_type=pl.DeviceIdType.MESH)
    for d in range(1, n_z):
        pl.semaphore_signal(barrier, inc=1, device_id=dev(c, lax.rem(z + d, n_z) * 2 + core), device_id_type=pl.DeviceIdType.MESH)
    pl.semaphore_signal(barrier, inc=1, device_id=dev(c, sibling), device_id_type=pl.DeviceIdType.MESH)
    pl.semaphore_wait(barrier, n_ctx + n_z - 1)

    def copy(src, dst, ss, rs, to):
        return pltpu.make_async_remote_copy(
            src_ref=src, dst_ref=dst, send_sem=ss, recv_sem=rs,
            device_id=to, device_id_type=pl.DeviceIdType.MESH)

    if square:
        cx = c + 1 - 2 * (c % 2)
        cy = lax.rem(c + 2, 4)
        cd = 3 - c
        direct = [cx, cy]
        others = [cx, cy, cd]
    else:
        direct = [lax.rem(c + d, n_ctx) for d in range(1, n_ctx)]
        others = direct
    pending = []

    kb[pl.ds(pl.multiple_of(c * rows, rows), rows), :] = k_ref[...]
    vb[pl.ds(pl.multiple_of(c * rows, rows), rows), :] = v_ref[...]
    pb[c] = prow_ref[...]

    def kv_copies(i, src, to):
        at = pl.ds(pl.multiple_of(src * rows, rows), rows)
        return [
            copy(kb.at[at], kb.at[at], kv_s.at[i, 0], kv_r.at[src, 0], to),
            copy(vb.at[at], vb.at[at], kv_s.at[i, 1], kv_r.at[src, 1], to),
            copy(pb.at[src], pb.at[src], kv_s.at[i, 2], kv_r.at[src, 2], to),
        ]

    for i, cc in enumerate(others):
        for cp in kv_copies(i, c, dev(cc, p)):
            cp.start()
            pending.append(cp)

    def piece(i, src, half):
        if i < 2:
            ref, buf = (wg_ref, wgb) if i == 0 else (wu_ref, wub)
            n = ref.shape[0]
            cols = pl.ds(0, ff)
        else:
            ref, buf = wd_ref, wdb
            n = ref.shape[0]
            cols = pl.ds((i - 2) * cw, cw)
        h = n // 2
        there = buf.at[pl.ds(pl.multiple_of(src * n + half * h, h), h), cols]
        return ref.at[pl.ds(half * h, h), cols], there

    def send_own(i):
        for order in range(2):
            for k, cc in enumerate(direct):
                half = order if k % 2 == 0 else 1 - order
                here, there = piece(i, c, half)
                cp = copy(here, there, w_s.at[i, k, half], w_r.at[i, c, half], dev(cc, p))
                cp.start()
                pending.append(cp)

    def arrived(i, src, half):
        _, there = piece(i, src, half)
        copy(there, there, w_s.at[i, 0, half], w_r.at[i, src, half], dev(direct[0], p)).wait_recv()

    def pass_on(i):
        if square:
            for src, half, to in ((cx, 0, cy), (cy, 1, cx)):
                arrived(i, src, half)
                _, there = piece(i, src, half)
                cp = copy(there, there, f_s.at[i, half], w_r.at[i, src, half], dev(to, p))
                cp.start()
                pending.append(cp)

    def finish(i):
        if square:
            for src, half in ((cx, 1), (cy, 0), (cd, 0), (cd, 1)):
                arrived(i, src, half)
        else:
            for src in direct:
                for half in range(2):
                    arrived(i, src, half)

    send_own(0)

    hid = hid_ref[...].astype(F32)
    scale = lax.rsqrt(jnp.mean(hid * hid, axis=-1, keepdims=True) + 1e-06)
    tok[z, core] = (hid * scale * gain_ref[...]).astype(BF16)
    eid = lax.broadcasted_iota(jnp.int32, (experts, toks), 0)
    named = jnp.zeros((experts, toks), F32)
    share = jnp.zeros((experts, toks), F32)
    for k in range(rt_ref.shape[0]):
        hit = rt_ref[k : k + 1, :] == eid
        named = jnp.where(hit, 1.0, named)
        share = jnp.where(hit, wt_ref[k : k + 1, :], share)
    before = (
        lax.broadcasted_iota(jnp.int32, (toks, toks), 0)
        < lax.broadcasted_iota(jnp.int32, (toks, toks), 1)
    ).astype(F32).astype(BF16)
    rank = jnp.dot(named.astype(BF16), before, preferred_element_type=F32)
    kept = (named > 0.5) & (rank < cap_ref[...].astype(F32))
    rb[z, core, :experts, :] = jnp.where(kept, rank, -1.0)
    rb[z, core, experts:, :] = jnp.where(kept, share, 0.0)

    def tok_copies(zz, cc, ss, rs, to):
        return (
            copy(tok.at[zz, cc], tok.at[zz, cc], ss.at[0], rs.at[0], to),
            copy(rb.at[zz, cc], rb.at[zz, cc], ss.at[1], rs.at[1], to),
        )

    def z_copies(d):
        to = dev(c, lax.rem(z + d, n_z) * 2 + core)
        return tok_copies(z, core, t_s.at[d], t_r.at[z], to)

    def z_arrivals(zz):
        return tok_copies(zz, core, t_s.at[0], t_r.at[zz], dev(c, sibling))

    def sib_copies(zz):
        return tok_copies(zz, core, u_s.at[zz], u_r.at[zz], dev(c, sibling))

    def sib_arrivals(zz):
        return tok_copies(zz, 1 - core, u_s.at[zz], u_r.at[zz], dev(c, sibling))

    @pl.loop(1, n_z)
    def _(d):
        for cp in z_copies(d):
            cp.start()

    for cp in sib_copies(z):
        cp.start()
    send_own(1)

    for src in others:
        for cp in kv_copies(0, src, dev(direct[0], p)):
            cp.wait_recv()
    key_pos = jnp.sum(pb[...], axis=0)[0:1, :]
    visible = key_pos <= pcol_ref[:, 0:1]
    bias = jnp.where(visible, 0.0, -jnp.inf)
    bias = jnp.concatenate([bias] * STACK, axis=0)
    per = HEADS // KVH
    for h0 in range(0, HEADS, STACK):
        g = h0 // per
        qs = jnp.concatenate([q_ref[:, (h0 + s) * HD : (h0 + s + 1) * HD] for s in range(STACK)], axis=0)
        sc = lax.dot_general(qs, kb[:, g * HD : (g + 1) * HD], (((1,), (1,)), ((), ())), preferred_element_type=F32)
        sc = sc * (1.0 / math.sqrt(HD)) + bias
        pr = jnp.exp(sc - jnp.max(sc, axis=-1, keepdims=True))
        total = jnp.sum(pr, axis=-1, keepdims=True)
        o = jnp.dot(pr.astype(BF16), vb[:, g * HD : (g + 1) * HD], preferred_element_type=F32) / total
        o = o.astype(BF16)
        for s in range(STACK):
            att_ref[:, (h0 + s) * HD : (h0 + s + 1) * HD] = o[s * rows : (s + 1) * rows]

    pass_on(0)

    def keep(ref, buf):
        n = ref.shape[0]
        buf[pl.ds(pl.multiple_of(c * n, n), n), :] = ref[...]

    keep(wg_ref, wgb)
    keep(wu_ref, wub)
    keep(wd_ref, wdb)
    pass_on(1)
    for i in range(CHUNKS):
        send_own(2 + i)

    slot_id = lax.broadcasted_iota(jnp.int32, (slots, toks), 0).astype(F32)

    def dispatch(zz, cc):
        hot = (rb[zz, cc, pl.ds(p, 1), :] == slot_id).astype(F32).astype(BF16)
        at = pl.ds(pl.multiple_of((zz * 2 + cc) * slots, slots), slots)
        xb[at, :] = jnp.dot(hot, tok[zz, cc], preferred_element_type=F32).astype(BF16)

    dispatch(z, core)

    @pl.loop(1, n_z)
    def _(d):
        zz = lax.rem(z + d, n_z)
        for cp in z_arrivals(zz):
            cp.wait_recv()
        for cp in sib_copies(zz):
            cp.start()
        dispatch(zz, core)

    @pl.loop(0, n_z)
    def _(d):
        zz = lax.rem(z + d, n_z)
        for cp in sib_arrivals(zz):
            cp.wait_recv()
        dispatch(zz, 1 - core)

    @pl.loop(1, n_z)
    def _(d):
        for cp in z_copies(d):
            cp.wait_send()

    @pl.loop(0, n_z)
    def _(d):
        for cp in sib_copies(d):
            cp.wait_send()

    ft = 256

    finish(0)

    @pl.loop(0, ff // ft)
    def _(t):
        at = pl.ds(pl.multiple_of(t * ft, ft), ft)
        gate = jnp.dot(xb[...], wgb[:, at], preferred_element_type=F32)
        gb[:, at] = gate / (1.0 + jnp.exp(-gate))

    finish(1)

    @pl.loop(0, ff // ft)
    def _(t):
        at = pl.ds(pl.multiple_of(t * ft, ft), ft)
        up = jnp.dot(xb[...], wub[:, at], preferred_element_type=F32)
        ab[:, at] = (gb[:, at] * up).astype(BF16)

    def combined(zz, cc):
        live = rb[zz, cc, pl.ds(p, 1), :] == slot_id
        weight = jnp.where(live, rb[zz, cc, pl.ds(experts + p, 1), :], 0.0)
        high = weight.astype(BF16)
        low = (weight - high.astype(F32)).astype(BF16)
        at = pl.ds(pl.multiple_of((zz * 2 + cc) * slots, slots), slots)
        y = yb[at, :]
        dims = (((0,), (0,)), ((), ()))
        return lax.dot_general(high, y, dims, preferred_element_type=F32) + lax.dot_general(
            low, y, dims, preferred_element_type=F32
        )

    def ret_copy(j, d):
        zz = lax.rem(z + d, n_z)
        cols = pl.ds(j * cw, cw)
        return copy(tok.at[zz, core, :, cols], ret.at[z, :, cols], r_s.at[j, d], r_r.at[j, z], dev(c, zz * 2 + core))

    def ret_arrival(j, d):
        zz = lax.rem(z + d, n_z)
        cols = pl.ds(j * cw, cw)
        return copy(tok.at[zz, core, :, cols], ret.at[zz, :, cols], r_s.at[j, d], r_r.at[j, zz], dev(c, zz * 2 + core))

    for j in range(CHUNKS):
        cols = pl.ds(j * cw, cw)
        pass_on(2 + j)
        finish(2 + j)
        for t in range(0, cw, ft):
            yb[:, t : t + ft] = jnp.dot(
                ab[...], wdb[:, j * cw + t : j * cw + t + ft], preferred_element_type=F32
            ).astype(BF16)

        @pl.loop(0, n_z)
        def _(zz):
            tok[zz, 1 - core, :, cols] = combined(zz, 1 - core).astype(BF16)

        pair = copy(tok.at[:, 1 - core, :, cols], sib.at[:, :, cols], s_s.at[j], s_r.at[j], dev(c, sibling))
        pair.start()
        pending.append(pair)
        own[:, cols] = combined(z, core)
        pair.wait_recv()

        @pl.loop(1, n_z)
        def _(d):
            zz = lax.rem(z + d, n_z)
            tok[zz, core, :, cols] = (combined(zz, core) + sib[zz, :, cols].astype(F32)).astype(BF16)
            ret_copy(j, d).start()

        own[:, cols] += sib[z, :, cols].astype(F32)

    for j in range(CHUNKS):
        cols = pl.ds(j * cw, cw)

        @pl.loop(1, n_z)
        def _(d):
            ret_arrival(j, d).wait_recv()
            own[:, cols] += ret[lax.rem(z + d, n_z), :, cols].astype(F32)

        mix_ref[:, cols] = (hid_ref[:, cols].astype(F32) + own[:, cols]).astype(BF16)

    for cp in pending:
        cp.wait_send()
    for j in range(CHUNKS):

        @pl.loop(1, n_z)
        def _(d):
            ret_copy(j, d).wait_send()


def body(query, keys, values, kept_pos, hidden, norm_gain, routes, route_weight, capacity, w_gate, w_up, w_down, n_ctx, n_ep):
    rows = query.shape[1]
    toks, width = hidden.shape
    topk = routes.shape[1]
    experts = capacity.shape[0]
    assert w_gate.shape[0] == 1
    cap = min(toks, max(2, 5 * toks * topk // (4 * experts)))
    slots = -(-cap // 16) * 16
    ff = w_gate.shape[2]
    n_z = n_ep // 2
    pieces = 2 + CHUNKS
    c = lax.axis_index("ctx")
    pos = kept_pos[0].astype(F32)
    lane = jnp.arange(n_ctx * rows) // rows
    prow = jnp.broadcast_to(jnp.where(lane == c, jnp.tile(pos, n_ctx), 0.0)[None], (8, n_ctx * rows))
    pcol = jnp.broadcast_to(pos[:, None], (rows, 128))
    capb = jnp.broadcast_to(capacity[:, None], (experts, toks))
    dma = pltpu.SemaphoreType.DMA
    vm = pl.BlockSpec(memory_space=pltpu.VMEM)
    attended, mixed = pl.pallas_call(
        functools.partial(kernel, n_ctx, n_ep, slots),
        out_shape=(
            jax.ShapeDtypeStruct((rows, query.shape[2]), BF16),
            jax.ShapeDtypeStruct((toks, width), BF16),
        ),
        in_specs=[vm] * 13,
        out_specs=(vm, vm),
        scratch_shapes=[
            pltpu.VMEM((n_ctx * rows, KVH * HD), BF16),
            pltpu.VMEM((n_ctx * rows, KVH * HD), BF16),
            pltpu.VMEM((n_ctx, 8, n_ctx * rows), F32),
            pltpu.VMEM((n_z, 2, toks, width), BF16),
            pltpu.VMEM((n_z, 2, 2 * experts, toks), F32),
            pltpu.VMEM((n_ep * slots, width), BF16),
            pltpu.VMEM((width, ff), BF16),
            pltpu.VMEM((width, ff), BF16),
            pltpu.VMEM((ff, width), BF16),
            pltpu.VMEM((n_ep * slots, ff), F32),
            pltpu.VMEM((n_ep * slots, ff), BF16),
            pltpu.VMEM((n_ep * slots, width // CHUNKS), BF16),
            pltpu.VMEM((n_z, toks, width), BF16),
            pltpu.VMEM((n_z, toks, width), BF16),
            pltpu.VMEM((toks, width), F32),
            dma((n_ctx, 3)),
            dma((n_ctx, 3)),
            dma((pieces, n_ctx, 2)),
            dma((pieces, n_ctx, 2)),
            dma((pieces, 2)),
            dma((n_z, 2)),
            dma((n_z, 2)),
            dma((n_z, 2)),
            dma((n_z, 2)),
            dma((CHUNKS,)),
            dma((CHUNKS,)),
            dma((CHUNKS, n_z)),
            dma((CHUNKS, n_z)),
        ],
        compiler_params=pltpu.CompilerParams(
            collective_id=0, has_side_effects=True, vmem_limit_bytes=62 * 1024 * 1024
        ),
    )(
        query[0], keys[0], values[0], prow, pcol, hidden, norm_gain[None], routes.T, route_weight.T, capb,
        w_gate[0], w_up[0], w_down[0],
    )
    return attended[None], mixed


def solution(mesh):
    placed = (
        P(("groups", "ep"), "ctx", None),
        P(("groups", "ep"), "ctx", None),
        P(("groups", "ep"), "ctx", None),
        P(("groups", "ep"), "ctx"),
        P(("groups", "ctx", "ep"), None),
        P(),
        P(("groups", "ctx", "ep"), None),
        P(("groups", "ctx", "ep"), None),
        P(),
        P("ep", "ctx", None),
        P("ep", "ctx", None),
        P("ep", "ctx", None),
    )
    return jax.shard_map(
        functools.partial(body, n_ctx=mesh.shape["ctx"], n_ep=mesh.shape["ep"]),
        mesh=mesh,
        in_specs=placed,
        out_specs=(P(("groups", "ep"), "ctx", None), P(("groups", "ctx", "ep"), None)),
        check_vma=False,
    )
```

time: 245 us -> 139 us (0.57)
  waiting for transfers between devices: 147 us -> 0 us
  Pallas kernels: 0 us -> 131 us
  blocking collectives: 23.4 us -> 0 us
  matrix products: 21.1 us -> 0 us
  between operations: 14.7 us -> 0.66 us
  local copies, waits for them, and re-layouts: 17.5 us -> 6.05 us
  starting transfers between devices: 11.2 us -> 0 us
  other arithmetic: 9.45 us -> 0.01 us
    pallas_call x0 -> x1, Pallas kernels: none -> 131 us  [body(): pl.pallas_call(functools.partial(kernel, n_ctx, n_ep, slots), out_shape=(...]
    all_to_all x2 -> x0, waiting for transfers between devices: 84.7 us -> none  [the longest x1 59.6 us: expert_section(): lax.all_to_all(outgoing, 'ep', split_axis=0, concat_axis=0, tiled=True)]
    all_gather x3 -> x0, waiting for transfers between devices: 60 us -> none  [the longest x1 45.9 us: body(): lax.all_gather(w_down, 'ctx', axis=1, tiled=True)]
    dot_general x5 -> x0, matrix products: 21.1 us -> none  [the longest x1 9.83 us: expert_section(): jnp.einsum('erf,efd->erd', hidden_act, full_down, preferred_element_type=...]
    all_gather x2 -> x0, blocking collectives: 15.9 us -> none  [the longest x1 8.41 us: attention_section(): key_piece = lax.all_gather(keys, 'ctx', axis=1, tiled=True)]
    all_to_all x2 -> x0, starting transfers between devices: 11.1 us -> none  [the longest x1 6.33 us: expert_section(): lax.all_to_all(outgoing, 'ep', split_axis=0, concat_axis=0, tiled=True)]
    convert_element_type x3 -> x0, local copies, waits for them, and re-layouts: 7.94 us -> none  [the longest x1 4.75 us: expert_section(): picked = flat_out[jnp.maximum(slot_of, 0)].astype(jnp.float32)]
    unnamed x1 -> x0, blocking collectives: 7.46 us -> none
  transfers between devices with their start and end apart: 5 -> 0, of which waited for: 4 -> 0; matrix products, arithmetic and copies ran while one was open for 10% -> 0% of each run, Pallas kernels for 0% -> 0%
where the time goes in v1:
time: 139 us; the launch traced here: 138 us
  Pallas kernels  131 us (94%)
  local copies, waits for them, and re-layouts  6.05 us (4%)
    pallas_call x1, Pallas kernels, body(): pl.pallas_call(functools.partial(kernel, n_ctx, n_ep, slots), out_shape=(...  131 us
    unnamed x8, local copies, waits for them, and re-layouts  4.02 us

profile of v1, /device:TPU:0, one launch (start us, length us, event | category | flops | bytes accessed | tf_op | source)
XLA Modules:
  0.0 137.5 jit_solution(2633855685160305270)
XLA Ops:
  0.6 0.0 copy-start.2
  0.6 0.6 copy-done.2
  1.3 0.1 tile.13
  1.4 0.0 copy-start.1
  1.4 0.6 copy-done.1
  2.0 0.7 broadcast_in_dim.32.cap_ref
  2.7 0.6 broadcast_in_dim.15.prow_ref
  3.3 0.7 broadcast_in_dim.30.pcol_ref
  4.0 130.8 %shard_map.131 = (bf16[64,4096]{1,0:T(8,128)(2,1)}, bf16[128,2048]{1,0:T(8,128)(2,1)}) custom-call(bf16[64,4096]{1,0:T(8,128)(2,1)} %bitcast.15, bf16[64,256]{1,0:T(8,128)(2,1)} %bitcast.17, bf16[64,256]{1,0:T(8,128)(2,1)} %bitcast.18, f32[8,256]{1,0:T(8,128)} %broadcast_in_dim.15.prow_ref, f32[64,128]{1,0:T(8,128)} %broadcast_in_dim.30.pcol_ref, ...), custom_call_target="tpu_custom_call" | custom-call | tf_op jit(solution)/shard_map/pallas_call | solution.py:351
  134.8 0.0 copy-start
  134.8 1.9 %copy.16 = bf16[1,64,4096]{2,1,0:T(8,128)(2,1)} copy(bf16[1,64,4096]{2,1,0:T(8,128)(2,1)} %bitcast.16) | data formatting | bytes 1048576
  136.7 0.0 copy-done
  136.7 0.8 copy.17
  (3 shorter events, 0.0 us)
Async XLA Ops:
  0.6 0.7 copy-start.2
  1.4 0.7 copy-start.1
  134.8 1.9 %copy-start = (bf16[128,2048]{1,0:T(8,128)(2,1)S(1)}, bf16[128,2048]{1,0:T(8,128)(2,1)}, u32[]{:S(2)}) copy-start(bf16[128,2048]{1,0:T(8,128)(2,1)} %get-tuple-element.9) | copy-start | bytes 1572868

commit v2 on v1

--- a/solution.py
+++ b/solution.py
@@ -19,11 +19,11 @@
 
 def kernel(
     n_ctx, n_ep, slots,
-    q_ref, k_ref, v_ref, prow_ref, pcol_ref, hid_ref, gain_ref, rt_ref, wt_ref, cap_ref,
+    q_ref, k_ref, v_ref, pos_ref, hid_ref, gain_ref, rt_ref, wt_ref, cap_ref,
     wg_ref, wu_ref, wd_ref,
     att_ref, mix_ref,
-    kb, vb, pb, tok, rb, xb, wgb, wub, wdb, gb, ab, yb, sib, ret, own,
-    kv_s, kv_r, w_s, w_r, f_s, t_s, t_r, u_s, u_r, s_s, s_r, r_s, r_r,
+    kb, vb, pb, tok, rb, xb, wgb, wub, wdb, gb, ab, yb, sib, ret, own, comb, rel,
+    kv_s, kv_r, w_s, w_r, f_s, t_s, t_r, u_s, u_r, s_s, s_r, r_s, r_r, l_s, x_s, x_r,
 ):
     gi = lax.axis_index("groups")
     c = lax.axis_index("ctx")
@@ -34,7 +34,7 @@
     square = n_ctx == 4
     rows = k_ref.shape[0]
     toks, width = hid_ref.shape
-    experts = cap_ref.shape[0]
+    experts = cap_ref.shape[1]
     ff = wg_ref.shape[1]
     cw = width // CHUNKS
 
@@ -67,7 +67,15 @@
 
     kb[pl.ds(pl.multiple_of(c * rows, rows), rows), :] = k_ref[...]
     vb[pl.ds(pl.multiple_of(c * rows, rows), rows), :] = v_ref[...]
-    pb[c] = prow_ref[...]
+    pos = pos_ref[...].astype(F32)
+    every = jnp.concatenate([pos] * n_ctx, axis=1)
+    lane = lax.broadcasted_iota(jnp.int32, (8, n_ctx * rows), 1)
+    pb[c] = jnp.where((lane >= c * rows) & (lane < (c + 1) * rows), every, 0.0)
+
+    def column(row):
+        n = row.shape[1]
+        diag = lax.broadcasted_iota(jnp.int32, (n, n), 0) == lax.broadcasted_iota(jnp.int32, (n, n), 1)
+        return jnp.sum(jnp.where(diag, row, 0.0), axis=1, keepdims=True)
 
     def kv_copies(i, src, to):
         at = pl.ds(pl.multiple_of(src * rows, rows), rows)
@@ -126,7 +134,14 @@
                 for half in range(2):
                     arrived(i, src, half)
 
+    def keep(i, ref, buf):
+        n = ref.shape[0]
+        return pltpu.make_async_copy(ref, buf.at[pl.ds(pl.multiple_of(c * n, n), n)], l_s.at[i])
+
+    local = [keep(0, wg_ref, wgb), keep(1, wu_ref, wub), keep(2, wd_ref, wdb)]
     send_own(0)
+    for cp in local:
+        cp.start()
 
     hid = hid_ref[...].astype(F32)
     scale = lax.rsqrt(jnp.mean(hid * hid, axis=-1, keepdims=True) + 1e-06)
@@ -143,7 +158,7 @@
         < lax.broadcasted_iota(jnp.int32, (toks, toks), 1)
     ).astype(F32).astype(BF16)
     rank = jnp.dot(named.astype(BF16), before, preferred_element_type=F32)
-    kept = (named > 0.5) & (rank < cap_ref[...].astype(F32))
+    kept = (named > 0.5) & (rank < column(cap_ref[...].astype(F32)))
     rb[z, core, :experts, :] = jnp.where(kept, rank, -1.0)
     rb[z, core, experts:, :] = jnp.where(kept, share, 0.0)
 
@@ -179,7 +194,7 @@
         for cp in kv_copies(0, src, dev(direct[0], p)):
             cp.wait_recv()
     key_pos = jnp.sum(pb[...], axis=0)[0:1, :]
-    visible = key_pos <= pcol_ref[:, 0:1]
+    visible = key_pos <= column(pos)
     bias = jnp.where(visible, 0.0, -jnp.inf)
     bias = jnp.concatenate([bias] * STACK, axis=0)
     per = HEADS // KVH
@@ -197,16 +212,7 @@
 
     pass_on(0)
 
-    def keep(ref, buf):
-        n = ref.shape[0]
-        buf[pl.ds(pl.multiple_of(c * n, n), n), :] = ref[...]
-
-    keep(wg_ref, wgb)
-    keep(wu_ref, wub)
-    keep(wd_ref, wdb)
     pass_on(1)
-    for i in range(CHUNKS):
-        send_own(2 + i)
 
     slot_id = lax.broadcasted_iota(jnp.int32, (slots, toks), 0).astype(F32)
 
@@ -214,6 +220,8 @@
         hot = (rb[zz, cc, pl.ds(p, 1), :] == slot_id).astype(F32).astype(BF16)
         at = pl.ds(pl.multiple_of((zz * 2 + cc) * slots, slots), slots)
         xb[at, :] = jnp.dot(hot, tok[zz, cc], preferred_element_type=F32).astype(BF16)
+        weight = jnp.where(rb[zz, cc, pl.ds(p, 1), :] == slot_id, rb[zz, cc, pl.ds(experts + p, 1), :], 0.0)
+        comb[zz, cc] = weight.T.astype(BF16)
 
     dispatch(z, core)
 
@@ -245,7 +253,10 @@
 
     ft = 256
 
+    for cp in local:
+        cp.wait()
     finish(0)
+    send_own(2)
 
     @pl.loop(0, ff // ft)
     def _(t):
@@ -254,6 +265,8 @@
         gb[:, at] = gate / (1.0 + jnp.exp(-gate))
 
     finish(1)
+    for j in range(1, min(3, CHUNKS)):
+        send_own(2 + j)
 
     @pl.loop(0, ff // ft)
     def _(t):
@@ -262,30 +275,37 @@
         ab[:, at] = (gb[:, at] * up).astype(BF16)
 
     def combined(zz, cc):
-        live = rb[zz, cc, pl.ds(p, 1), :] == slot_id
-        weight = jnp.where(live, rb[zz, cc, pl.ds(experts + p, 1), :], 0.0)
-        high = weight.astype(BF16)
-        low = (weight - high.astype(F32)).astype(BF16)
         at = pl.ds(pl.multiple_of((zz * 2 + cc) * slots, slots), slots)
-        y = yb[at, :]
-        dims = (((0,), (0,)), ((), ()))
-        return lax.dot_general(high, y, dims, preferred_element_type=F32) + lax.dot_general(
-            low, y, dims, preferred_element_type=F32
-        )
-
-    def ret_copy(j, d):
-        zz = lax.rem(z + d, n_z)
+        return jnp.dot(comb[zz, cc], yb[at, :], preferred_element_type=F32)
+
+    line = n_z == 4
+    low = z == 0
+    high = z == 3
+    end = low | high
+    if line:
+        first = jnp.where(low, 2, jnp.where(high, 1, z - 1))
+        second = jnp.where(low, 1, jnp.where(high, 2, z + 1))
+        far = jnp.where(z < 2, 3, 0)
+        inner = jnp.where(z < 2, 1, 2)
+
+    def ret_copy(j, zz):
         cols = pl.ds(j * cw, cw)
-        return copy(tok.at[zz, core, :, cols], ret.at[z, :, cols], r_s.at[j, d], r_r.at[j, z], dev(c, zz * 2 + core))
-
-    def ret_arrival(j, d):
-        zz = lax.rem(z + d, n_z)
+        return copy(tok.at[zz, core, :, cols], ret.at[z, :, cols], r_s.at[j, zz], r_r.at[j, z], dev(c, zz * 2 + core))
+
+    def ret_arrival(j, zz):
         cols = pl.ds(j * cw, cw)
-        return copy(tok.at[zz, core, :, cols], ret.at[zz, :, cols], r_s.at[j, d], r_r.at[j, zz], dev(c, zz * 2 + core))
-
+        return copy(tok.at[zz, core, :, cols], ret.at[zz, :, cols], r_s.at[j, zz], r_r.at[j, zz], dev(c, zz * 2 + core))
+
+    def relay(j):
+        cols = pl.ds(j * cw, cw)
+        return copy(tok.at[far, core, :, cols], rel.at[:, cols], x_s.at[j], x_r.at[j], dev(c, inner * 2 + core))
+
+    def part(j, zz):
+        return combined(zz, core) + sib[zz, :, j * cw : (j + 1) * cw].astype(F32)
+
+    pass_on(2)
     for j in range(CHUNKS):
         cols = pl.ds(j * cw, cw)
-        pass_on(2 + j)
         finish(2 + j)
         for t in range(0, cw, ft):
             yb[:, t : t + ft] = jnp.dot(
@@ -299,34 +319,83 @@
         pair = copy(tok.at[:, 1 - core, :, cols], sib.at[:, :, cols], s_s.at[j], s_r.at[j], dev(c, sibling))
         pair.start()
         pending.append(pair)
+        if j + 3 < CHUNKS:
+            send_own(2 + j + 3)
         own[:, cols] = combined(z, core)
         pair.wait_recv()
-
-        @pl.loop(1, n_z)
-        def _(d):
-            zz = lax.rem(z + d, n_z)
-            tok[zz, core, :, cols] = (combined(zz, core) + sib[zz, :, cols].astype(F32)).astype(BF16)
-            ret_copy(j, d).start()
+        if line:
+
+            @pl.when(end)
+            def _():
+                tok[far, core, :, cols] = part(j, far).astype(BF16)
+                relay(j).start()
+
+            for zz in (first, second):
+                tok[zz, core, :, cols] = part(j, zz).astype(BF16)
+                ret_copy(j, zz).start()
+
+            @pl.when(jnp.logical_not(end))
+            def _():
+                mine = part(j, far)
+                relay(j).wait_recv()
+                tok[far, core, :, cols] = (mine + rel[:, cols].astype(F32)).astype(BF16)
+                ret_copy(j, far).start()
+
+        else:
+
+            @pl.loop(1, n_z)
+            def _(d):
+                zz = lax.rem(z + d, n_z)
+                tok[zz, core, :, cols] = part(j, zz).astype(BF16)
+                ret_copy(j, zz).start()
 
         own[:, cols] += sib[z, :, cols].astype(F32)
+        if j + 1 < CHUNKS:
+            pass_on(2 + j + 1)
 
     for j in range(CHUNKS):
         cols = pl.ds(j * cw, cw)
 
-        @pl.loop(1, n_z)
-        def _(d):
-            ret_arrival(j, d).wait_recv()
-            own[:, cols] += ret[lax.rem(z + d, n_z), :, cols].astype(F32)
+        def take(zz):
+            ret_arrival(j, zz).wait_recv()
+            own[:, cols] += ret[zz, :, cols].astype(F32)
+
+        if line:
+            for zz in (first, second):
+                take(jnp.where(end, 3 - zz, zz))
+
+            @pl.when(jnp.logical_not(end))
+            def _():
+                take(far)
+
+        else:
+
+            @pl.loop(1, n_z)
+            def _(d):
+                take(lax.rem(z + d, n_z))
 
         mix_ref[:, cols] = (hid_ref[:, cols].astype(F32) + own[:, cols]).astype(BF16)
 
     for cp in pending:
         cp.wait_send()
     for j in range(CHUNKS):
-
-        @pl.loop(1, n_z)
-        def _(d):
-            ret_copy(j, d).wait_send()
+        if line:
+            for zz in (first, second):
+                ret_copy(j, zz).wait_send()
+
+            @pl.when(end)
+            def _():
+                relay(j).wait_send()
+
+            @pl.when(jnp.logical_not(end))
+            def _():
+                ret_copy(j, far).wait_send()
+
+        else:
+
+            @pl.loop(1, n_z)
+            def _(d):
+                ret_copy(j, lax.rem(z + d, n_z)).wait_send()
 
 
 def body(query, keys, values, kept_pos, hidden, norm_gain, routes, route_weight, capacity, w_gate, w_up, w_down, n_ctx, n_ep):
@@ -340,12 +409,6 @@
     ff = w_gate.shape[2]
     n_z = n_ep // 2
     pieces = 2 + CHUNKS
-    c = lax.axis_index("ctx")
-    pos = kept_pos[0].astype(F32)
-    lane = jnp.arange(n_ctx * rows) // rows
-    prow = jnp.broadcast_to(jnp.where(lane == c, jnp.tile(pos, n_ctx), 0.0)[None], (8, n_ctx * rows))
-    pcol = jnp.broadcast_to(pos[:, None], (rows, 128))
-    capb = jnp.broadcast_to(capacity[:, None], (experts, toks))
     dma = pltpu.SemaphoreType.DMA
     vm = pl.BlockSpec(memory_space=pltpu.VMEM)
     attended, mixed = pl.pallas_call(
@@ -354,7 +417,7 @@
             jax.ShapeDtypeStruct((rows, query.shape[2]), BF16),
             jax.ShapeDtypeStruct((toks, width), BF16),
         ),
-        in_specs=[vm] * 13,
+        in_specs=[vm] * 9 + [pl.BlockSpec(memory_space=pl.ANY)] * 3,
         out_specs=(vm, vm),
         scratch_shapes=[
             pltpu.VMEM((n_ctx * rows, KVH * HD), BF16),
@@ -372,6 +435,8 @@
             pltpu.VMEM((n_z, toks, width), BF16),
             pltpu.VMEM((n_z, toks, width), BF16),
             pltpu.VMEM((toks, width), F32),
+            pltpu.VMEM((n_z, 2, toks, slots), BF16),
+            pltpu.VMEM((toks, width), BF16),
             dma((n_ctx, 3)),
             dma((n_ctx, 3)),
             dma((pieces, n_ctx, 2)),
@@ -385,12 +450,15 @@
             dma((CHUNKS,)),
             dma((CHUNKS, n_z)),
             dma((CHUNKS, n_z)),
+            dma((3,)),
+            dma((CHUNKS,)),
+            dma((CHUNKS,)),
         ],
         compiler_params=pltpu.CompilerParams(
             collective_id=0, has_side_effects=True, vmem_limit_bytes=62 * 1024 * 1024
         ),
     )(
-        query[0], keys[0], values[0], prow, pcol, hidden, norm_gain[None], routes.T, route_weight.T, capb,
+        query[0], keys[0], values[0], kept_pos, hidden, norm_gain[None], routes.T, route_weight.T, capacity[None],
         w_gate[0], w_up[0], w_down[0],
     )
     return attended[None], mixed

time: 139 us -> 126 us (0.906)
  Pallas kernels: 131 us -> 122 us
  local copies, waits for them, and re-layouts: 6.05 us -> 2.72 us
    pallas_call x1, Pallas kernels: 131 us -> 122 us  [body(): pl.pallas_call(functools.partial(kernel, n_ctx, n_ep, slots), out_shape=(...]
    broadcast_in_dim x3 -> x0, local copies, waits for them, and re-layouts: 1.94 us -> none  [the longest x1 0.69 us: body(): pcol = jnp.broadcast_to(pos[:, None], (rows, 128))]
    unnamed x8 -> x4, local copies, waits for them, and re-layouts: 4.02 us -> 2.72 us
where the time goes in v2:
time: 126 us; the launch traced here: 125 us
  Pallas kernels  122 us (97%)
  local copies, waits for them, and re-layouts  2.72 us (2%)
    pallas_call x1, Pallas kernels, body(): pl.pallas_call(functools.partial(kernel, n_ctx, n_ep, slots), out_shape=(...  122 us
    unnamed x4, local copies, waits for them, and re-layouts  2.72 us

profile of v2, /device:TPU:0, one launch (start us, length us, event | category | flops | bytes accessed | tf_op | source)
XLA Modules:
  0.0 125.5 jit_solution(10770656541004751237)
XLA Ops:
  0.6 122.1 %shard_map.131 = (bf16[64,4096]{1,0:T(8,128)(2,1)}, bf16[128,2048]{1,0:T(8,128)(2,1)}) custom-call(bf16[64,4096]{1,0:T(8,128)(2,1)} %bitcast.14, bf16[64,256]{1,0:T(8,128)(2,1)} %bitcast.16, bf16[64,256]{1,0:T(8,128)(2,1)} %bitcast.17, s32[1,64]{1,0:T(1,128)} %pos_ref.1, bf16[128,2048]{1,0:T(8,128)(2,1)} %hid_ref.1, f32[1,2048]{1,0:T(1,128)} %bitcast.18, ...), custom_call_target="tpu_custom_call" | custom-call | tf_op jit(solution)/shard_map/pallas_call | solution.py:414
  122.7 0.0 copy-start
  122.7 1.9 %copy.16 = bf16[1,64,4096]{2,1,0:T(8,128)(2,1)} copy(bf16[1,64,4096]{2,1,0:T(8,128)(2,1)} %bitcast.15) | data formatting | bytes 1048576
  124.7 0.0 copy-done
  124.7 0.8 copy.17
Async XLA Ops:
  122.7 1.9 %copy-start = (bf16[128,2048]{1,0:T(8,128)(2,1)S(1)}, bf16[128,2048]{1,0:T(8,128)(2,1)}, u32[]{:S(2)}) copy-start(bf16[128,2048]{1,0:T(8,128)(2,1)} %get-tuple-element.9) | copy-start | bytes 1572868
